TPU v7x, 32 devices: a whole 2x2x4 slice. The times are simulated.
32 devices in a mesh: groups: 2 (over x), seq: 16 (over z, y, core).
Axes of the slice: x: 2, y: 2, z: 4, core: 2. Of those that a mesh axis runs over, the one named last changes fastest.
Arguments:
- tokens: bfloat16 [32768, 2048], P(('groups', 'seq')), parts along dimension 0, may hold values from -64 to 64, as said below
- gain_mix: float32 [2048], replicated, may hold values from 0.1 to 1.9
- gain_mlp: float32 [2048], replicated, may hold values from 0.1 to 1.9
- block_mix: bfloat16 [1024, 1024], replicated, may hold values from -0.1875 to 0.1875
- cross_mix: bfloat16 [16, 16], replicated, may hold values from -1.5 to 1.5
- w_in: bfloat16 [2048, 1024], P('seq'), may hold values from -0.25 to 0.25
- w_out: bfloat16 [4096, 512], P('seq'), may hold values from -0.1875 to 0.1875
Outputs:
- mixed: bfloat16 [32768, 2048], P(('groups', 'seq')), parts along dimension 0
There are 2 independent parts, one for each index of `groups`. A program takes and returns all parts, laid end to end along the dimension named above; an argument that names none is the same for every part. Nothing has to cross between parts.
Inputs may be any that keep to these rules, and one draw needn't show every extreme that they name: `tokens`: activations with independent scales per channel and per position.
All inputs are finite; a program needn't handle non-finite values.
Results may differ from a plain program's by a relative error of at most 0.0085.
Values may be sent and summed in bfloat16 or wider, within the bound.
A program may use at most 128 MiB of HBM per device.

v0:
```python
import jax
import jax.numpy as jnp
from jax import lax
from jax.sharding import PartitionSpec as P

NCB = 4
BLK = 1024


def rms_scale(values, gain):
    mean_square = jnp.mean(values * values, axis=-1, keepdims=True)
    return values * lax.rsqrt(mean_square + 1e-06) * gain


def shards(tokens, gain_mix, gain_mlp, block_mix, cross_mix, w_in, w_out):
    rows, width = tokens.shape
    nblocks = rows // BLK
    raw = tokens.astype(jnp.float32)
    normed = rms_scale(raw, gain_mix).astype(jnp.bfloat16)
    within = jnp.einsum(
        "hp,ops->ohs",
        block_mix,
        normed.reshape(nblocks, BLK, width),
        preferred_element_type=jnp.float32,
    ).astype(jnp.bfloat16)
    mixed_cols = jnp.einsum(
        "ai,ijd->ajd",
        cross_mix,
        lax.all_to_all(within, "seq", split_axis=1, concat_axis=0, tiled=True),
        preferred_element_type=jnp.float32,
    ).astype(jnp.bfloat16)
    across = lax.all_to_all(mixed_cols, "seq", split_axis=0, concat_axis=1, tiled=True)
    gated = (
        raw + normed.astype(jnp.float32) * across.reshape(rows, width).astype(jnp.float32)
    ).astype(jnp.bfloat16)
    inner = rms_scale(gated.astype(jnp.float32), gain_mlp).astype(jnp.bfloat16)
    weight_in = lax.all_gather(w_in, "seq", axis=0, tiled=True)
    hidden = jnp.einsum(
        "rcd,cdf->rcf",
        inner.reshape(rows, NCB, width // NCB),
        weight_in.reshape(NCB, width // NCB, -1),
        preferred_element_type=jnp.float32,
    )
    hidden = jax.nn.gelu(hidden).astype(jnp.bfloat16)
    weight_out = lax.all_gather(w_out, "seq", axis=0, tiled=True)
    output = jnp.einsum(
        "rcf,cfd->rcd",
        hidden,
        weight_out.reshape(NCB, hidden.shape[2], -1),
        preferred_element_type=jnp.float32,
    )
    return (gated.astype(jnp.float32) + output.reshape(rows, width)).astype(jnp.bfloat16)


def solution(mesh):
    in_specs = (P(("groups", "seq"), None), P(), P(), P(), P(), P("seq", None), P("seq", None))
    out_specs = P(("groups", "seq"), None)
    return jax.shard_map(shards, mesh=mesh, in_specs=in_specs, out_specs=out_specs, check_vma=False)
```

profile of v0, /device:TPU:13, one launch (start us, length us, event | category | flops | bytes accessed | tf_op | source)
XLA Modules:
  0.0 401.5 jit_solution(3762509726161138529)
XLA Ops:
  6.5 3.2 fusion.8
  9.8 9.2 %convert_bitcast_fusion.1 = bf16[1,1024,2048]{1,2,0:T(8,128)(2,1)} fusion(bf16[1024,1024]{1,0:T(8,128)(2,1)S(1)} %copy-done, bf16[1024,2048]{1,0:T(8,128)(2,1)} %param.7, f32[2048]{0:T(1024)} %param.8, f32[1024]{0:T(1024)S(1)} %add_rsqrt_fusion.1), kind=kOutput, calls=%fused_computation.29 | convolution fusion | flops 4305453056 | bytes 10498048 | tf_op jit(solution)/shard_map/hp,ops->ohs/dot_general | solution.py:20
  19.0 20.6 %copy.17 = bf16[1,1024,2048]{2,0,1:T(2,128)(2,1)} copy(bf16[1,1024,2048]{1,2,0:T(8,128)(2,1)} %convert_bitcast_fusion.1) | data formatting | bytes 8388608 | tf_op jit(solution)/shard_map/convert_element_type | solution.py:25
  39.6 0.5 broadcast.36
  40.2 26.7 %reduce = bf16[1024,2048]{1,0:T(8,128)(2,1)} reduce(bf16[1024,1,2048]{2,1,0:T(2,128)(2,1)} %bitcast.34, bf16[]{:T(256)} %broadcast.36), dimensions={1}, to_apply=%bitcast.28.reduce_sub_computation | reduce | bytes 8388610
  66.9 11.4 %reshape.51 = bf16[16,2,65536]{2,1,0:T(2,128)(2,1)} reshape(bf16[1024,2048]{1,0:T(8,128)(2,1)} %reduce) | data formatting | bytes 8388608
  78.3 6.6 %all-to-all-start = ((bf16[16,2,65536]{2,1,0:T(2,128)(2,1)}), bf16[16,2,65536]{2,1,0:T(2,128)(2,1)}, u32[]{:S(2)}, u32[]{:S(2)}) async-start(bf16[16,2,65536]{2,1,0:T(2,128)(2,1)} %reshape.51), calls=%async_computation | async-start | bytes 8388608 | tf_op jit(solution)/shard_map/all_to_all | solution.py:29
  84.8 0.2 all-gather.3.cloned.1.call-start
  85.0 0.5 all-gather.3.cloned.1.call-update
  85.5 117.0 %all-to-all-done = bf16[16,2,65536]{2,1,0:T(2,128)(2,1)} async-done(((bf16[16,2,65536]{2,1,0:T(2,128)(2,1)}), bf16[16,2,65536]{2,1,0:T(2,128)(2,1)}, u32[]{:S(2)}, u32[]{:S(2)}) %all-to-all-start) | async-done | bytes 4194336 | tf_op jit(solution)/shard_map/all_to_all | solution.py:29
  202.6 12.4 %reshape.52 = bf16[1024,1,2048]{2,1,0:T(2,128)(2,1)} reshape(bf16[16,2,65536]{2,1,0:T(2,128)(2,1)} %all-to-all-done) | data formatting | bytes 8388608
  214.9 6.0 %copy.24 = bf16[1,1024,2048]{2,1,0:T(8,128)(2,1)S(1)} copy(bf16[1,1024,2048]{2,0,1:T(2,128)(2,1)} %bitcast.35) | data formatting | bytes 8388608
  221.0 4.8 %convert_bitcast_fusion = bf16[16,64,2048]{2,0,1:T(8,128)(2,1)S(1)} fusion(bf16[16,64,2048]{2,1,0:T(8,128)(2,1)S(1)} %bitcast.36, bf16[16,16]{1,0:T(8,128)(2,1)S(1)} %copy-done.5), kind=kOutput, calls=%fused_computation.28 | convolution fusion | flops 69206016 | bytes 8389120 | tf_op jit(solution)/shard_map/ai,ijd->ajd/dot_general | solution.py:26
  225.8 4.3 %copy.19 = bf16[16,64,2048]{2,1,0:T(8,128)(2,1)} copy(bf16[16,64,2048]{2,0,1:T(8,128)(2,1)S(1)} %convert_bitcast_fusion) | data formatting | bytes 8388608 | tf_op jit(solution)/shard_map/convert_element_type | solution.py:31
  230.1 4.9 %all-to-all-start.1 = ((bf16[16,64,2048]{2,1,0:T(8,128)(2,1)}), bf16[16,64,2048]{2,1,0:T(8,128)(2,1)}, u32[]{:S(2)}, u32[]{:S(2)}) async-start(bf16[16,64,2048]{2,1,0:T(8,128)(2,1)} %copy.19), calls=%async_computation.1 | async-start | bytes 8388608 | tf_op jit(solution)/shard_map/all_to_all | solution.py:32
  235.0 0.3 all-gather.5.cloned.1.call-start
  235.3 0.5 all-gather.5.cloned.1.call-update
  235.8 117.0 %all-to-all-done.1 = bf16[16,64,2048]{2,1,0:T(8,128)(2,1)} async-done(((bf16[16,64,2048]{2,1,0:T(8,128)(2,1)}), bf16[16,64,2048]{2,1,0:T(8,128)(2,1)}, u32[]{:S(2)}, u32[]{:S(2)}) %all-to-all-start.1) | async-done | bytes 4194336 | tf_op jit(solution)/shard_map/all_to_all | solution.py:32
  352.8 5.0 %fusion.12 = (f32[1024]{0:T(1024)S(1)}, bf16[1024,2048]{1,0:T(8,128)(2,1)S(1)}) fusion(bf16[16,64,2048]{2,1,0:T(8,128)(2,1)} %all-to-all-done.1, f32[2048]{0:T(1024)S(1)} %copy-done.3, f32[1024]{0:T(1024)S(1)} %add_rsqrt_fusion.1, bf16[1024,2048]{1,0:T(8,128)(2,1)} %param.7), kind=kLoop, calls=%fused_computation.19 | loop fusion | flops 25164800 | bytes 12599296 | tf_op jit(solution)/shard_map/reduce_sum | solution.py:11
  357.8 1.9 copy-done.2
  359.7 3.0 fusion.14
  362.7 14.3 %fusion.28 = f32[4,1024,512]{1,2,0:T(8,128)} fusion(bf16[4,1024,512]{2,1,0:T(8,128)(2,1)} %bitcast.40, bf16[4,512,1024]{2,1,0:T(8,128)(2,1)} %bitcast.39, bf16[128,4,8,512]{3,2,1,0:T(8,128)(2,1)} %bitcast.38), kind=kOutput, calls=%fused_computation.32 | convolution fusion | flops 8627683328 | bytes 20971520 | tf_op jit(solution)/shard_map/rcf,cfd->rcd/dot_general | solution.py:46
  377.1 9.3 %copy.22 = f32[1024,2048]{1,0:T(8,128)} copy(f32[1024,2048]{0,1:T(8,128)} %bitcast.37) | data formatting | bytes 16777216 | tf_op jit(solution)/shard_map/reshape | solution.py:52
  386.4 8.3 %fusion.15 = bf16[1024,2048]{1,0:T(8,128)(2,1)} fusion(f32[1024,2048]{1,0:T(8,128)} %copy.22, bf16[1024,2048]{1,0:T(8,128)(2,1)} %copy-done.2), kind=kLoop, calls=%fused_computation.22 | loop fusion | flops 6291456 | bytes 16777216 | tf_op jit(solution)/shard_map/convert_element_type | solution.py:52
  (15 shorter events, 0.0 us)
Async XLA Ops:
  6.5 3.2 copy-start
  78.3 124.3 %all-to-all-start = ((bf16[16,2,65536]{2,1,0:T(2,128)(2,1)}), bf16[16,2,65536]{2,1,0:T(2,128)(2,1)}, u32[]{:S(2)}, u32[]{:S(2)}) async-start(bf16[16,2,65536]{2,1,0:T(2,128)(2,1)} %reshape.51), calls=%async_computation | async-start | bytes 8388608 | tf_op jit(solution)/shard_map/all_to_all | solution.py:29
  84.8 277.9 %all-gather.3.cloned.1.call-start = ((), (), s32[]{:S(2)}) async-start(), calls=%async_computation.2 | async-start | bytes 4456448 | tf_op jit(solution)/shard_map/all_gather | solution.py:37
  214.9 6.0 %copy-start.5 = (bf16[16,16]{1,0:T(8,128)(2,1)S(1)}, bf16[16,16]{1,0:T(8,128)(2,1)}, u32[]{:S(2)}) copy-start(bf16[16,16]{1,0:T(8,128)(2,1)} %param.11) | copy-start | bytes 1540
  225.8 127.0 %copy-start.3 = (f32[2048]{0:T(1024)S(1)}, f32[2048]{0:T(1024)}, u32[]{:S(2)}) copy-start(f32[2048]{0:T(1024)} %param.8) | copy-start | bytes 24580
  230.1 122.7 %all-to-all-start.1 = ((bf16[16,64,2048]{2,1,0:T(8,128)(2,1)}), bf16[16,64,2048]{2,1,0:T(8,128)(2,1)}, u32[]{:S(2)}, u32[]{:S(2)}) async-start(bf16[16,64,2048]{2,1,0:T(8,128)(2,1)} %copy.19), calls=%async_computation.1 | async-start | bytes 8388608 | tf_op jit(solution)/shard_map/all_to_all | solution.py:32
  235.0 124.7 %copy-start.4 = (f32[2048]{0:T(1024)S(1)}, f32[2048]{0:T(1024)}, u32[]{:S(2)}) copy-start(f32[2048]{0:T(1024)} %param.9) | copy-start | bytes 24580
  235.0 127.7 %all-gather.5.cloned.1.call-start = ((), (), s32[]{:S(2)}) async-start(), calls=%async_computation.3 | async-start | bytes 4456448 | tf_op jit(solution)/shard_map/all_gather | solution.py:45
  357.8 1.9 copy-start.2
  377.1 17.6 %copy-start.1 = (bf16[1024,1024]{1,0:T(8,128)(2,1)S(1)}, bf16[1024,1024]{1,0:T(8,128)(2,1)}, u32[]{:S(2)}) copy-start(bf16[1024,1024]{1,0:T(8,128)(2,1)} %param.10) | copy-start | bytes 6291460
Sparse Core Ops, SparseCore 0:
  87.8 94.8 all-gather.2
  238.0 94.8 all-gather.4
where the time goes:
time: 403 us; the launch traced here: 402 us
  waiting for transfers between devices  235 us (58%)
  local copies, waits for them, and re-layouts  66.5 us (17%)
  other arithmetic  46.3 us (11%)
  matrix products  28.3 us (7%)
  between operations  13.5 us (3%)
  starting transfers between devices  11.9 us (3%)
    all_to_all x1, waiting for transfers between devices, shards(): lax.all_to_all(within, 'seq', split_axis=1, concat_axis=0, tiled=True)  117 us
    all_to_all x1, waiting for transfers between devices, shards(): lax.all_to_all(mixed_cols, 'seq', split_axis=0, concat_axis=1, tiled=True)  117 us
    unnamed x16, local copies, waits for them, and re-layouts  32.2 us
    unnamed x1, other arithmetic  26.7 us
    convert_element_type x1, local copies, waits for them, and re-layouts, shards(): within = jnp.einsum('hp,ops->ohs', block_mix, normed.reshape(nblocks, BLK...  20.6 us
    dot_general x1, matrix products, shards(): jnp.einsum('rcf,cfd->rcd', hidden, weight_out.reshape(NCB, hidden.shape[2...  14.3 us
    reshape x1, local copies, waits for them, and re-layouts, shards(): output.reshape(rows, width)  9.34 us
    dot_general x1, matrix products, shards(): jnp.einsum('hp,ops->ohs', block_mix, normed.reshape(nblocks, BLK, width),...  9.21 us
  transfers between devices with their start and end apart: 4, of which 2 were waited for; matrix products, arithmetic and copies ran while one was open for 9% of the time, Pallas kernels for 0%

commit v1 on v0

v1 whole, which is shorter than its diff:
```python
import jax
import jax.numpy as jnp
from jax import lax
from jax.experimental import pallas as pl
from jax.experimental.pallas import tpu as pltpu
from jax.sharding import PartitionSpec as P

NCB = 4
BLK = 1024
CHUNKS = 8
LANES = 128
SUB = 16
MESH = pl.DeviceIdType.MESH
BF16 = jnp.bfloat16
F32 = jnp.float32


def kernel(
    n, tokens, gain_mix, gain_mlp, block_mix, cross_mix, w_in, w_out, out,
    tok, normed, mat, win, wout, send1, got1, send2, got2, kron, gated, inner, result,
    load_sem, mat_sem, own_sem, line_send, line_recv, hop_send, hop_recv,
    s1, r1, s2, r2, out_sem,
):
    width = tokens.shape[1]
    part = BLK // CHUNKS
    col_groups = width // LANES
    row_groups = n // col_groups
    rows = part // row_groups
    line = n // 4
    x = lax.axis_index("groups")
    me = lax.axis_index("seq")
    at, lane = me // 4, me % 4
    y, core = lane // 2, lane % 2

    def rows_of(g):
        return pl.ds(pl.multiple_of(g * part, part), part)

    def load(g):
        return pltpu.make_async_copy(tokens.at[rows_of(g)], tok.at[rows_of(g)], load_sem.at[g])

    @pl.loop(0, CHUNKS)
    def _(g):
        load(g).start()

    load_mat = pltpu.make_async_copy(block_mix, mat, mat_sem)
    load_mat.start()

    barrier = pltpu.get_barrier_semaphore()

    @pl.loop(1, n)
    def _(k):
        pl.semaphore_signal(barrier, inc=1, device_id=(x, (me + k) % n), device_id_type=MESH)

    pl.semaphore_signal(barrier, inc=1, device_id=(1 - x, me), device_id_type=MESH)
    pl.semaphore_wait(barrier, n)

    def by_kind(fn):
        @pl.when(x == 0)
        def _():
            fn(w_in, win)

        @pl.when(x == 1)
        def _():
            fn(w_out, wout)

    def line_copy(full, t, way):
        shard = at - t if way == 0 else at + t
        to = at + 1 if way == 0 else at - 1
        return pltpu.make_async_remote_copy(
            src_ref=full.at[shard, lane], dst_ref=full.at[shard, lane],
            send_sem=line_send.at[way, t], recv_sem=line_recv.at[way, t],
            device_id=(x, to * 4 + lane), device_id_type=MESH,
        )

    def line_start(t):
        def go(_, full):
            @pl.when((at < line - 1) & (at - t >= 0))
            def _():
                line_copy(full, t, 0).start()

            @pl.when((at > 0) & (at + t <= line - 1))
            def _():
                line_copy(full, t, 1).start()
        by_kind(go)

    def line_arrived(t):
        def go(_, full):
            @pl.when(at - 1 - t >= 0)
            def _():
                block = full.at[at - 1 - t, lane]
                pltpu.make_async_copy(block, block, line_recv.at[0, t]).wait()

            @pl.when(at + 1 + t <= line - 1)
            def _():
                block = full.at[at + 1 + t, lane]
                pltpu.make_async_copy(block, block, line_recv.at[1, t]).wait()
        by_kind(go)

    def line_sent(t):
        def go(_, full):
            @pl.when((at < line - 1) & (at - t >= 0))
            def _():
                line_copy(full, t, 0).wait_send()

            @pl.when((at > 0) & (at + t <= line - 1))
            def _():
                line_copy(full, t, 1).wait_send()
        by_kind(go)

    def hop(full, which, slot, device):
        return pltpu.make_async_remote_copy(
            src_ref=full.at[:, which], dst_ref=full.at[:, which],
            send_sem=hop_send.at[slot], recv_sem=hop_recv.at[slot],
            device_id=device, device_id_type=MESH,
        )

    def arrived(full, which, slot):
        block = full.at[:, which]
        pltpu.make_async_copy(block, block, hop_recv.at[slot]).wait()

    over_y = (1 - y) * 2 + core
    over_c = y * 2 + 1 - core
    over_yc = (1 - y) * 2 + 1 - core
    peer_y = (x, at * 4 + over_y)
    peer_x = (1 - x, me)
    peer_c = (x, at * 4 + over_c)

    def own(shard, full):
        return pltpu.make_async_copy(shard, full.at[at, lane], own_sem)

    by_kind(lambda shard, full: own(shard, full).start())
    by_kind(lambda shard, full: own(shard, full).wait())
    line_start(0)

    big = n * SUB
    pick = (lax.broadcasted_iota(jnp.int32, (big, n), 0) // SUB
            == lax.broadcasted_iota(jnp.int32, (big, n), 1)).astype(BF16)
    spread = jnp.dot(pick, cross_mix[...], preferred_element_type=F32).astype(BF16)
    spread = lax.dot_general(spread, pick, (((1,), (1,)), ((), ())), preferred_element_type=F32)
    same = (lax.broadcasted_iota(jnp.int32, (big, big), 0) % SUB
            == lax.broadcasted_iota(jnp.int32, (big, big), 1) % SUB)
    kron[...] = jnp.where(same, spread, 0.0).astype(BF16)

    tile = 32

    @pl.loop(0, CHUNKS)
    def _(g):
        load(g).wait()

        @pl.loop(0, part // tile)
        def _(i):
            at_rows = pl.ds(pl.multiple_of(g * part + i * tile, tile), tile)
            raw = tok[at_rows, :].astype(F32)
            mean_square = jnp.mean(raw * raw, axis=-1, keepdims=True)
            normed[at_rows, :] = (raw * lax.rsqrt(mean_square + 1e-06) * gain_mix[...]).astype(BF16)

    load_mat.wait()
    line_arrived(0)
    for t in range(1, 2):
        line_start(t)

    bits = []
    while (1 << len(bits)) < n:
        b = 1 << len(bits)
        bits.append((b, (1 - 2 * ((me // b) % 2)) * b))

    def partner(k):
        q = me
        for b, step in bits:
            q = q + ((k // b) % 2) * step
        return q

    def exchange(src, dst, g, send_sem, recv_sem):
        pltpu.make_async_copy(src.at[g, me], dst.at[g, me], recv_sem.at[g]).start()

        @pl.loop(1, n)
        def _(k):
            q = partner(n - k)
            pltpu.make_async_remote_copy(
                src_ref=src.at[g, q], dst_ref=dst.at[g, me],
                send_sem=send_sem.at[g], recv_sem=recv_sem.at[g],
                device_id=(x, q), device_id_type=MESH,
            ).start()

    def wait_all(ref, g, sem):
        pltpu.make_async_copy(ref.at[g], ref.at[g], sem.at[g]).wait()

    def wait_sent(ref, g, sem):
        block = ref.at[g, pl.ds(0, n - 1)]
        pltpu.make_async_copy(block, block, sem.at[g]).wait()

    def mix_positions(g):
        left = mat[rows_of(g), :]

        @pl.loop(0, width // 256)
        def _(j):
            res = jnp.dot(left, normed[:, pl.ds(pl.multiple_of(j * 256, 256), 256)],
                          preferred_element_type=F32).astype(BF16)
            for r in range(row_groups):
                for c in range(2):
                    send1[g, r * col_groups + 2 * j + c] = res[
                        r * rows:(r + 1) * rows, c * LANES:(c + 1) * LANES]
        exchange(send1, got1, g, s1, r1)

    def weights_2():
        for t in range(1, line - 1):
            line_arrived(t)
            if t + 1 < line - 1:
                line_start(t + 1)

    def weights_3():
        by_kind(lambda _, full: hop(full, lane, 0, peer_y).start())

    def weights_4():
        by_kind(lambda _, full: arrived(full, over_y, 0))

        def go(_, full):
            hop(full, lane, 1, peer_x).start()
            hop(full, over_y, 2, peer_x).start()
        by_kind(go)

    def from_x(x_kind):
        full = wout if x_kind == 0 else win
        arrived(full, lane, 1)
        arrived(full, over_y, 2)

    def weights_5():
        @pl.when(x == 0)
        def _():
            from_x(0)

        @pl.when(x == 1)
        def _():
            from_x(1)
        hop(win, lane, 3, peer_c).start()
        hop(win, over_y, 4, peer_c).start()
        hop(wout, lane, 5, peer_c).start()
        hop(wout, over_y, 6, peer_c).start()

    @pl.loop(0, CHUNKS)
    def _(g):
        mix_positions(g)
        pl.when(g == 1)(weights_2)
        pl.when(g == 2)(weights_3)
        pl.when(g == 5)(weights_4)

    pair = 2 if rows % (2 * SUB) == 0 else 1

    @pl.loop(0, CHUNKS)
    def _(g):
        wait_all(got1, g, r1)
        for t in range(rows // (SUB * pair)):
            cuts = [slice((t * pair + p) * SUB, (t * pair + p + 1) * SUB) for p in range(pair)]
            parts = [got1[g, :, cut, :].reshape(big, LANES) for cut in cuts]
            joined = parts[0] if pair == 1 else jnp.concatenate(parts, axis=1)
            res = jnp.dot(kron[...], joined, preferred_element_type=F32).astype(BF16)
            for p in range(pair):
                send2[g, :, cuts[p], :] = res[:, p * LANES:(p + 1) * LANES].reshape(n, SUB, LANES)
        exchange(send2, got2, g, s2, r2)
        pl.when(g == 2)(weights_5)

    arrived(win, over_c, 3)
    arrived(win, over_yc, 4)
    arrived(wout, over_c, 5)
    arrived(wout, over_yc, 6)

    depth = width // NCB
    hidden_width = w_in.shape[-1]
    per = line // NCB
    small = min(rows, 32)

    def store(g):
        return pltpu.make_async_copy(result.at[rows_of(g)], out.at[rows_of(g)], out_sem.at[g])

    @pl.loop(0, CHUNKS)
    def _(g):
        wait_all(got2, g, r2)

        for i in range(part // small):
            r, inside = divmod(i * small, rows)
            cut = slice(i * small, (i + 1) * small)
            at_rows = pl.ds(pl.multiple_of(g * part + i * small, small), small)
            mixed = jnp.concatenate(
                [got2[g, r * col_groups + c, inside:inside + small, :] for c in range(col_groups)], axis=1)
            gate = (tok[at_rows, :].astype(F32)
                    + normed[at_rows, :].astype(F32) * mixed.astype(F32)).astype(BF16)
            gated[cut, :] = gate
            wide = gate.astype(F32)
            mean_square = jnp.mean(wide * wide, axis=-1, keepdims=True)
            inner[cut, :] = (wide * lax.rsqrt(mean_square + 1e-06) * gain_mlp[...]).astype(BF16)

        for b in range(NCB):
            cols = slice(b * depth, (b + 1) * depth)
            first = win[b * per:(b + 1) * per].reshape(depth, hidden_width)
            hidden = jnp.dot(inner[:, cols], first, preferred_element_type=F32)
            hidden = jax.nn.gelu(hidden).astype(BF16)
            second = wout[b * per:(b + 1) * per].reshape(hidden_width, depth)
            res = jnp.dot(hidden, second, preferred_element_type=F32)
            result[rows_of(g), cols] = (gated[:, cols].astype(F32) + res).astype(BF16)
        store(g).start()

    for t in range(line - 1):
        line_sent(t)
    by_kind(lambda _, full: hop(full, lane, 0, peer_y).wait_send())

    def sent_x(_, full):
        hop(full, lane, 1, peer_x).wait_send()
        hop(full, over_y, 2, peer_x).wait_send()
    by_kind(sent_x)
    hop(win, lane, 3, peer_c).wait_send()
    hop(win, over_y, 4, peer_c).wait_send()
    hop(wout, lane, 5, peer_c).wait_send()
    hop(wout, over_y, 6, peer_c).wait_send()

    @pl.loop(0, CHUNKS)
    def _(g):
        wait_sent(send1, g, s1)
        wait_sent(send2, g, s2)
        store(g).wait()


def make(n):
    def shards(tokens, gain_mix, gain_mlp, block_mix, cross_mix, w_in, w_out):
        count, width = tokens.shape
        part = BLK // CHUNKS
        rows = part // (n // (width // LANES))
        line = n // 4
        vmem = pl.BlockSpec(memory_space=pltpu.VMEM)
        hbm = pl.BlockSpec(memory_space=pl.ANY)
        dma = pltpu.SemaphoreType.DMA
        block = pltpu.VMEM((CHUNKS, n, rows, LANES), BF16)
        whole = pltpu.VMEM((count, width), BF16)
        def body(*refs):
            kernel(n, *refs)
        return pl.pallas_call(
            body,
            out_shape=jax.ShapeDtypeStruct((count, width), BF16),
            in_specs=[hbm, vmem, vmem, hbm, vmem, hbm, hbm],
            out_specs=hbm,
            scratch_shapes=[
                whole, whole, pltpu.VMEM((BLK, BLK), BF16),
                pltpu.VMEM((line, 4) + w_in.shape, BF16),
                pltpu.VMEM((line, 4) + w_out.shape, BF16),
                block, block, block, block,
                pltpu.VMEM((n * SUB, n * SUB), BF16),
                pltpu.VMEM((part, width), BF16), pltpu.VMEM((part, width), BF16), whole,
                dma((CHUNKS,)), dma(()), dma(()), dma((2, line)), dma((2, line)), dma((7,)), dma((7,)),
                dma((CHUNKS,)), dma((CHUNKS,)), dma((CHUNKS,)), dma((CHUNKS,)), dma((CHUNKS,)),
            ],
            compiler_params=pltpu.CompilerParams(
                collective_id=0, has_side_effects=True, vmem_limit_bytes=58 * 1024 * 1024),
        )(tokens, gain_mix.reshape(1, -1), gain_mlp.reshape(1, -1), block_mix, cross_mix, w_in, w_out)
    return shards


def solution(mesh):
    in_specs = (P(("groups", "seq"), None), P(), P(), P(), P(), P("seq", None), P("seq", None))
    out_specs = P(("groups", "seq"), None)
    return jax.shard_map(make(mesh.shape["seq"]), mesh=mesh, in_specs=in_specs, out_specs=out_specs, check_vma=False)
```

time: 403 us -> 211 us (0.52)
  the two profiles are of different devices: /device:TPU:13 before, /device:TPU:0 now
where the time goes in v1:
time: 211 us
  Pallas kernels  206 us (98%)
  local copies, waits for them, and re-layouts  4.79 us (2%)
    pallas_call x1, Pallas kernels, shards(): pl.pallas_call(body, out_shape=jax.ShapeDtypeStruct((count, width), BF16)...  206 us
    unnamed x1, local copies, waits for them, and re-layouts  4.79 us

profile of v1, /device:TPU:0, one launch (start us, length us, event | category | flops | bytes accessed | tf_op | source)
XLA Modules:
  0.0 210.6 jit_solution(203460920933067006)
XLA Ops:
  0.0 205.8 %shard_map.73 = bf16[1024,2048]{1,0:T(8,128)(2,1)} custom-call(bf16[1024,2048]{1,0:T(8,128)(2,1)} %refs_0_.1, f32[1,2048]{1,0:T(1,128)} %bitcast.2, f32[1,2048]{1,0:T(1,128)} %bitcast.3, bf16[1024,1024]{1,0:T(8,128)(2,1)} %refs_3_.1, bf16[16,16]{1,0:T(8,128)(2,1)} %refs_4_.1, bf16[128,1024]{1,0:T(8,128)(2,1)} %refs_5_.1, bf16[256,512]{1,0:T(8,128)(2,1)} %refs_6_.1), custom_call_target="tpu_custom_call" | custom-call | tf_op jit(solution)/shard_map/pallas_call | solution.py:335
  205.8 4.8 %copy.9 = bf16[1024,2048]{1,0:T(8,128)(2,1)} copy(bf16[1024,2048]{1,0:T(8,128)(2,1)} %shard_map.73) | data formatting | bytes 8388608

commit v2 on v1

--- a/solution.py
+++ b/solution.py
@@ -38,13 +38,6 @@
     def load(g):
         return pltpu.make_async_copy(tokens.at[rows_of(g)], tok.at[rows_of(g)], load_sem.at[g])
 
-    @pl.loop(0, CHUNKS)
-    def _(g):
-        load(g).start()
-
-    load_mat = pltpu.make_async_copy(block_mix, mat, mat_sem)
-    load_mat.start()
-
     barrier = pltpu.get_barrier_semaphore()
 
     @pl.loop(1, n)
@@ -52,7 +45,13 @@
         pl.semaphore_signal(barrier, inc=1, device_id=(x, (me + k) % n), device_id_type=MESH)
 
     pl.semaphore_signal(barrier, inc=1, device_id=(1 - x, me), device_id_type=MESH)
-    pl.semaphore_wait(barrier, n)
+    @pl.loop(0, CHUNKS)
+    def _(g):
+        load(g).start()
+
+    load_mat = pltpu.make_async_copy(block_mix, mat, mat_sem)
+    load_mat.start()
+
 
     def by_kind(fn):
         @pl.when(x == 0)
@@ -63,24 +62,24 @@
         def _():
             fn(w_out, wout)
 
-    def line_copy(full, t, way):
+    def line_copy(mine, full, t, way):
         shard = at - t if way == 0 else at + t
         to = at + 1 if way == 0 else at - 1
         return pltpu.make_async_remote_copy(
-            src_ref=full.at[shard, lane], dst_ref=full.at[shard, lane],
+            src_ref=mine if t == 0 else full.at[shard, lane], dst_ref=full.at[shard, lane],
             send_sem=line_send.at[way, t], recv_sem=line_recv.at[way, t],
             device_id=(x, to * 4 + lane), device_id_type=MESH,
         )
 
     def line_start(t):
-        def go(_, full):
+        def go(mine, full):
             @pl.when((at < line - 1) & (at - t >= 0))
             def _():
-                line_copy(full, t, 0).start()
+                line_copy(mine, full, t, 0).start()
 
             @pl.when((at > 0) & (at + t <= line - 1))
             def _():
-                line_copy(full, t, 1).start()
+                line_copy(mine, full, t, 1).start()
         by_kind(go)
 
     def line_arrived(t):
@@ -97,14 +96,14 @@
         by_kind(go)
 
     def line_sent(t):
-        def go(_, full):
+        def go(mine, full):
             @pl.when((at < line - 1) & (at - t >= 0))
             def _():
-                line_copy(full, t, 0).wait_send()
+                line_copy(mine, full, t, 0).wait_send()
 
             @pl.when((at > 0) & (at + t <= line - 1))
             def _():
-                line_copy(full, t, 1).wait_send()
+                line_copy(mine, full, t, 1).wait_send()
         by_kind(go)
 
     def hop(full, which, slot, device):
@@ -127,10 +126,6 @@
 
     def own(shard, full):
         return pltpu.make_async_copy(shard, full.at[at, lane], own_sem)
-
-    by_kind(lambda shard, full: own(shard, full).start())
-    by_kind(lambda shard, full: own(shard, full).wait())
-    line_start(0)
 
     big = n * SUB
     pick = (lax.broadcasted_iota(jnp.int32, (big, n), 0) // SUB
@@ -141,6 +136,10 @@
             == lax.broadcasted_iota(jnp.int32, (big, big), 1) % SUB)
     kron[...] = jnp.where(same, spread, 0.0).astype(BF16)
 
+    pl.semaphore_wait(barrier, n)
+    by_kind(lambda shard, full: own(shard, full).start())
+    line_start(0)
+
     tile = 32
 
     @pl.loop(0, CHUNKS)
@@ -155,9 +154,6 @@
             normed[at_rows, :] = (raw * lax.rsqrt(mean_square + 1e-06) * gain_mix[...]).astype(BF16)
 
     load_mat.wait()
-    line_arrived(0)
-    for t in range(1, 2):
-        line_start(t)
 
     bits = []
     while (1 << len(bits)) < n:
@@ -175,7 +171,7 @@
 
         @pl.loop(1, n)
         def _(k):
-            q = partner(n - k)
+            q = partner(k)
             pltpu.make_async_remote_copy(
                 src_ref=src.at[g, q], dst_ref=dst.at[g, me],
                 send_sem=send_sem.at[g], recv_sem=recv_sem.at[g],
@@ -209,6 +205,7 @@
                 line_start(t + 1)
 
     def weights_3():
+        by_kind(lambda shard, full: own(shard, full).wait())
         by_kind(lambda _, full: hop(full, lane, 0, peer_y).start())
 
     def weights_4():
@@ -240,9 +237,16 @@
     @pl.loop(0, CHUNKS)
     def _(g):
         mix_positions(g)
-        pl.when(g == 1)(weights_2)
-        pl.when(g == 2)(weights_3)
-        pl.when(g == 5)(weights_4)
+
+        @pl.when(g == 0)
+        def _():
+            line_arrived(0)
+            line_start(1)
+
+        @pl.when(g == 1)
+        def _():
+            weights_2()
+            weights_3()
 
     pair = 2 if rows % (2 * SUB) == 0 else 1
 
@@ -257,7 +261,8 @@
             for p in range(pair):
                 send2[g, :, cuts[p], :] = res[:, p * LANES:(p + 1) * LANES].reshape(n, SUB, LANES)
         exchange(send2, got2, g, s2, r2)
-        pl.when(g == 2)(weights_5)
+        pl.when(g == 0)(weights_4)
+        pl.when(g == CHUNKS // 2)(weights_5)
 
     arrived(win, over_c, 3)
     arrived(win, over_yc, 4)
@@ -317,6 +322,18 @@
         wait_sent(send1, g, s1)
         wait_sent(send2, g, s2)
         store(g).wait()
+
+
+def write_out(result, out, in_sem, out_sem, held):
+    part = result.shape[0] // CHUNKS
+    cuts = [pl.ds(g * part, part) for g in range(CHUNKS)]
+    for g, cut in enumerate(cuts):
+        pltpu.make_async_copy(result.at[cut], held.at[cut], in_sem.at[g]).start()
+    for g, cut in enumerate(cuts):
+        pltpu.make_async_copy(result.at[cut], held.at[cut], in_sem.at[g]).wait()
+        pltpu.make_async_copy(held.at[cut], out.at[cut], out_sem.at[g]).start()
+    for g, cut in enumerate(cuts):
+        pltpu.make_async_copy(held.at[cut], out.at[cut], out_sem.at[g]).wait()
 
 
 def make(n):
@@ -332,7 +349,7 @@
         whole = pltpu.VMEM((count, width), BF16)
         def body(*refs):
             kernel(n, *refs)
-        return pl.pallas_call(
+        result = pl.pallas_call(
             body,
             out_shape=jax.ShapeDtypeStruct((count, width), BF16),
             in_specs=[hbm, vmem, vmem, hbm, vmem, hbm, hbm],
@@ -350,6 +367,14 @@
             compiler_params=pltpu.CompilerParams(
                 collective_id=0, has_side_effects=True, vmem_limit_bytes=58 * 1024 * 1024),
         )(tokens, gain_mix.reshape(1, -1), gain_mlp.reshape(1, -1), block_mix, cross_mix, w_in, w_out)
+        return pl.pallas_call(
+            write_out,
+            out_shape=jax.ShapeDtypeStruct((count, width), BF16),
+            in_specs=[hbm],
+            out_specs=hbm,
+            scratch_shapes=[dma((CHUNKS,)), dma((CHUNKS,)), whole],
+            compiler_params=pltpu.CompilerParams(vmem_limit_bytes=16 * 1024 * 1024),
+        )(result)
     return shards
 
 

time: 211 us -> 207 us (0.981)
  the two profiles are of different devices: /device:TPU:0 before, /device:TPU:13 now
where the time goes in v2:
time: 207 us; the launch traced here: 206 us
  Pallas kernels  204 us (99%)
  local copies, waits for them, and re-layouts  2.18 us (1%)
    pallas_call x1, Pallas kernels, shards(): pl.pallas_call(body, out_shape=jax.ShapeDtypeStruct((count, width), BF16)...  201 us

profile of v2, /device:TPU:13, one launch (start us, length us, event | category | flops | bytes accessed | tf_op | source)
XLA Modules:
  0.0 206.1 jit_solution(1734024745502359044)
XLA Ops:
  0.0 201.5 %shard_map.73.result = bf16[1024,2048]{1,0:T(8,128)(2,1)} custom-call(bf16[1024,2048]{1,0:T(8,128)(2,1)} %refs_0_.1, f32[1,2048]{1,0:T(1,128)} %bitcast.2, f32[1,2048]{1,0:T(1,128)} %bitcast.3, bf16[1024,1024]{1,0:T(8,128)(2,1)} %refs_3_.1, bf16[16,16]{1,0:T(8,128)(2,1)} %refs_4_.1, bf16[128,1024]{1,0:T(8,128)(2,1)} %refs_5_.1, bf16[256,512]{1,0:T(8,128)(2,1)} %refs_6_.1), custom_call_target="tpu_custom_call" | custom-call | tf_op jit(solution)/shard_map/pallas_call | solution.py:352
  201.5 0.0 copy-start
  201.5 2.2 %copy-done = bf16[1024,2048]{1,0:T(8,128)(2,1)S(1)} copy-done((bf16[1024,2048]{1,0:T(8,128)(2,1)S(1)}, bf16[1024,2048]{1,0:T(8,128)(2,1)}, u32[]{:S(2)}) %copy-start) | copy-done | bytes 4194328
  203.7 2.4 %shard_map.74 = bf16[1024,2048]{1,0:T(8,128)(2,1)} custom-call(bf16[1024,2048]{1,0:T(8,128)(2,1)S(1)} %copy-done), custom_call_target="tpu_custom_call" | custom-call | tf_op jit(solution)/shard_map/pallas_call | solution.py:370
Async XLA Ops:
  201.5 2.2 %copy-start = (bf16[1024,2048]{1,0:T(8,128)(2,1)S(1)}, bf16[1024,2048]{1,0:T(8,128)(2,1)}, u32[]{:S(2)}) copy-start(bf16[1024,2048]{1,0:T(8,128)(2,1)} %shard_map.73.result) | copy-start | bytes 12582916

commit v3 on v2

--- a/solution.py
+++ b/solution.py
@@ -136,10 +136,6 @@
             == lax.broadcasted_iota(jnp.int32, (big, big), 1) % SUB)
     kron[...] = jnp.where(same, spread, 0.0).astype(BF16)
 
-    pl.semaphore_wait(barrier, n)
-    by_kind(lambda shard, full: own(shard, full).start())
-    line_start(0)
-
     tile = 32
 
     @pl.loop(0, CHUNKS)
@@ -153,6 +149,9 @@
             mean_square = jnp.mean(raw * raw, axis=-1, keepdims=True)
             normed[at_rows, :] = (raw * lax.rsqrt(mean_square + 1e-06) * gain_mix[...]).astype(BF16)
 
+    pl.semaphore_wait(barrier, n)
+    by_kind(lambda shard, full: own(shard, full).start())
+    line_start(0)
     load_mat.wait()
 
     bits = []

time: 207 us -> 210 us (1.014)
    pallas_call x1, Pallas kernels: 201 us -> 204 us  [shards(): pl.pallas_call(body, out_shape=jax.ShapeDtypeStruct((count, width), BF16)...]
where the time goes in v3:
time: 210 us; the launch traced here: 208 us
  Pallas kernels  206 us (98%)
  local copies, waits for them, and re-layouts  2.18 us (1%)
    pallas_call x1, Pallas kernels, shards(): pl.pallas_call(body, out_shape=jax.ShapeDtypeStruct((count, width), BF16)...  204 us

profile of v3, /device:TPU:13, one launch (start us, length us, event | category | flops | bytes accessed | tf_op | source)
XLA Modules:
  0.0 208.3 jit_solution(6012418651144242506)
XLA Ops:
  0.0 203.6 %shard_map.73.result = bf16[1024,2048]{1,0:T(8,128)(2,1)} custom-call(bf16[1024,2048]{1,0:T(8,128)(2,1)} %refs_0_.1, f32[1,2048]{1,0:T(1,128)} %bitcast.2, f32[1,2048]{1,0:T(1,128)} %bitcast.3, bf16[1024,1024]{1,0:T(8,128)(2,1)} %refs_3_.1, bf16[16,16]{1,0:T(8,128)(2,1)} %refs_4_.1, bf16[128,1024]{1,0:T(8,128)(2,1)} %refs_5_.1, bf16[256,512]{1,0:T(8,128)(2,1)} %refs_6_.1), custom_call_target="tpu_custom_call" | custom-call | tf_op jit(solution)/shard_map/pallas_call | solution.py:351
  203.6 0.0 copy-start
  203.7 2.2 %copy-done = bf16[1024,2048]{1,0:T(8,128)(2,1)S(1)} copy-done((bf16[1024,2048]{1,0:T(8,128)(2,1)S(1)}, bf16[1024,2048]{1,0:T(8,128)(2,1)}, u32[]{:S(2)}) %copy-start) | copy-done | bytes 4194328
  205.8 2.4 %shard_map.74 = bf16[1024,2048]{1,0:T(8,128)(2,1)} custom-call(bf16[1024,2048]{1,0:T(8,128)(2,1)S(1)} %copy-done), custom_call_target="tpu_custom_call" | custom-call | tf_op jit(solution)/shard_map/pallas_call | solution.py:369
Async XLA Ops:
  203.6 2.2 %copy-start = (bf16[1024,2048]{1,0:T(8,128)(2,1)S(1)}, bf16[1024,2048]{1,0:T(8,128)(2,1)}, u32[]{:S(2)}) copy-start(bf16[1024,2048]{1,0:T(8,128)(2,1)} %shard_map.73.result) | copy-start | bytes 12582916
